TPU v7x, 256 devices: a whole 4x4x8 slice. The times are simulated.
256 devices in a mesh: group: 8 (over x_hi, y), layer: 32 (over z, x_lo, core).
Axes of the slice: x: 4 (x_hi: 2, x_lo: 2; x = x_hi * 2 + x_lo), y: 4, z: 8, core: 2. Of those that a mesh axis runs over, the one named last changes fastest.
Arguments:
- query_grads: bfloat16 [1024, 131072], P('group', 'layer'), may hold values from -6 to 6
- query_ids: int32 [1024], P('group'), may hold values from 0 to 1023, each once
- train_feats: bfloat16 [8192, 131072], P('group', 'layer'), may hold values from -6 to 6
- basis_out: float32 [32, 64, 64], P('layer'), may hold values from -0.75 to 0.75
- basis_in: float32 [32, 64, 64], P('layer'), may hold values from -0.75 to 0.75
- eigen_vals: float32 [32, 64, 64], P('layer'), may hold values from 0.2 to 5
Outputs:
- scores: float32 [1024, 8192], P('layer', 'group')
Inputs may be any that keep to these rules, and one draw needn't show every extreme that they name: `query_ids`: each number of 0 to 1023 appears exactly once.
All inputs are finite; a program needn't handle non-finite values.
Results may differ from a plain program's by a relative error of at most 0.0029.
Values may be sent and summed in bfloat16 or wider, within the bound.
A program may use at most 64 MiB of HBM per device.

v0:
```python
import math

import jax
import jax.numpy as jnp
from jax import lax
from jax.sharding import PartitionSpec as P

damping = 0.1


def from_behind(block, axis, distance):
    devices = range(lax.axis_size(axis))
    route = [((i - distance) % len(devices), i) for i in devices]
    return lax.ppermute(block, axis, route)


def precondition(grads, basis_out, basis_in, eigen_vals):
    width = basis_out.shape[-1]
    square = grads.reshape(grads.shape[0], width, width).astype(jnp.float32)
    rotated = jnp.einsum(
        "ai,qab,bj->qij", basis_out, square, basis_in, precision=lax.Precision.HIGHEST
    )
    scaled = rotated / (eigen_vals + damping)
    restored = jnp.einsum(
        "ai,qij,bj->qab", basis_out, scaled, basis_in, precision=lax.Precision.HIGHEST
    )
    return restored.reshape(grads.shape[0], width * width).astype(jnp.bfloat16)


def on_device(query_grads, query_ids, train_feats, basis_out, basis_in, eigen_vals):
    group_count = lax.axis_size("group")
    layer_count = lax.axis_size("layer")
    prepared = precondition(query_grads, basis_out[0], basis_in[0], eigen_vals[0])
    query_total = query_grads.shape[0] * group_count
    empty = jnp.zeros((query_total, train_feats.shape[0]), jnp.float32)

    def place_tile(partial_value, query_block, block_ids):
        score_tile = jnp.einsum(
            "qf,tf->qt", query_block, train_feats, preferred_element_type=jnp.float32
        )
        return partial_value.at[block_ids].set(score_tile)

    def cycle_step(index, state_tuple):
        partial_value, query_block, block_ids = state_tuple
        partial_value = place_tile(partial_value, query_block, block_ids)
        query_block, block_ids = from_behind((query_block, block_ids), "group", 1)
        return (partial_value, query_block, block_ids)

    partial_value, query_block, block_ids = lax.fori_loop(
        0, group_count - 1, cycle_step, (empty, prepared, query_ids)
    )
    partial_value = place_tile(partial_value, query_block, block_ids)
    summed = lax.psum_scatter(partial_value, "layer", scatter_dimension=0, tiled=True)
    scale = 1.0 / math.sqrt(layer_count * prepared.shape[1])
    return summed * scale


def solution(mesh):
    return jax.shard_map(
        on_device,
        mesh=mesh,
        in_specs=(
            P("group", "layer"),
            P("group"),
            P("group", "layer"),
            P("layer", None, None),
            P("layer", None, None),
            P("layer", None, None),
        ),
        out_specs=P("layer", "group"),
        check_vma=False,
    )
```

profile of v0, /device:TPU:1, one launch (start us, length us, event | category | flops | bytes accessed | tf_op | source)
XLA Modules:
  0.0 361.3 jit_solution(3936270639604970070)
XLA Ops:
  8.9 3.5 copy.17
  12.5 6.1 %fusion.7 = f32[128,64,64]{1,2,0:T(8,128)S(1)} fusion(bf16[128,64,64]{1,2,0:T(8,128)(2,1)S(1)} %copy.17, f32[1,64,64]{2,1,0:T(8,128)S(1)} %copy-done), kind=kOutput, calls=%fused_computation.12 | convolution fusion | flops 402653184 | bytes 3162112 | tf_op jit(solution)/shard_map/ai,qab,bj->qij/dot_general | solution.py:20
  18.6 3.6 fusion.4
  22.2 8.2 %fusion = f32[128,64,64]{2,1,0:T(8,128)} fusion(f32[128,64,64]{2,1,0:T(8,128)S(1)} %fusion.4, f32[64,64]{1,0:T(8,128)S(1)} %add_bitcast_fusion, f32[1,64,64]{2,1,0:T(8,128)S(1)} %copy-done), kind=kOutput, calls=%fused_computation.3 | convolution fusion | flops 403177472 | bytes 4227072 | tf_op jit(solution)/shard_map/ai,qij,bj->qab/dot_general | solution.py:24
  30.4 4.5 %copy.20 = f32[128,64,64]{0,1,2:T(8,128)S(1)} copy(f32[128,64,64]{2,1,0:T(8,128)} %fusion) | data formatting | bytes 4194304 | tf_op jit(solution)/shard_map/ai,qij,bj->qab/dot_general | solution.py:24
  40.0 164.9 %while.14 = (s32[]{:T(128)}, f32[1024,1024]{1,0:T(8,128)}, bf16[128,4096]{1,0:T(8,128)(2,1)S(1)}, s32[128]{0:T(128)S(1)}, bf16[1024,4096]{1,0:T(8,128)(2,1)}, /*index=5*/s32[]{:T(128)}) while((s32[]{:T(128)}, f32[1024,1024]{1,0:T(8,128)}, bf16[128,4096]{1,0:T(8,128)(2,1)S(1)}, s32[128]{0:T(128)S(1)}, bf16[1024,4096]{1,0:T(8,128)(2,1)}, ...), condition=%wide.region_2.0_spmd, body=%wide.region_0.0_spmd.sunk | while | flops 1073742208 | bytes 17830548 | solution.py:49
  43.6 6.3 %fusion.23 = f32[128,1024]{1,0:T(8,128)S(1)} fusion(bf16[128,4096]{1,0:T(8,128)(2,1)S(1)} %copy.31, bf16[1024,4096]{1,0:T(8,128)(2,1)} %get-tuple-element.114), kind=kOutput, calls=%fused_computation.16.clone.1 | convolution fusion | flops 1073741824 | bytes 9961472 | tf_op jit(solution)/shard_map/while/body/eval_jaxpr/qf,tf->qt/dot_general | solution.py:38
  49.8 5.1 %scatter_fusion = f32[1024,1024]{1,0:T(8,128)} fusion(f32[1024,1024]{1,0:T(8,128)} %get-tuple-element.105, s32[128]{0:T(128)S(1)} %compare_select_fusion.3, f32[128,1024]{1,0:T(8,128)S(1)} %fusion.23), kind=kCustom, calls=%fused_computation.clone.1 | custom fusion | bytes 1573376 | tf_op jit(solution)/shard_map/while/body/eval_jaxpr/scatter | solution.py:41
  54.9 12.1 %collective-permute-done.1 = s32[128]{0:T(128)S(1)} collective-permute-done((s32[128]{0:T(128)S(1)}, s32[128]{0:T(128)S(1)}, u32[]{:S(2)}, u32[]{:S(2)}) %collective-permute-start.1) | collective-permute-done | bytes 544 | tf_op jit(solution)/shard_map/while/body/eval_jaxpr/ppermute | solution.py:14
  67.8 6.3 %fusion.23 = f32[128,1024]{1,0:T(8,128)S(1)} fusion(bf16[128,4096]{1,0:T(8,128)(2,1)S(1)} %copy.31, bf16[1024,4096]{1,0:T(8,128)(2,1)} %get-tuple-element.114), kind=kOutput, calls=%fused_computation.16.clone.1 | convolution fusion | flops 1073741824 | bytes 9961472 | tf_op jit(solution)/shard_map/while/body/eval_jaxpr/qf,tf->qt/dot_general | solution.py:38
  74.0 5.1 %scatter_fusion = f32[1024,1024]{1,0:T(8,128)} fusion(f32[1024,1024]{1,0:T(8,128)} %get-tuple-element.105, s32[128]{0:T(128)S(1)} %compare_select_fusion.3, f32[128,1024]{1,0:T(8,128)S(1)} %fusion.23), kind=kCustom, calls=%fused_computation.clone.1 | custom fusion | bytes 1573376 | tf_op jit(solution)/shard_map/while/body/eval_jaxpr/scatter | solution.py:41
  79.1 13.1 %collective-permute-done.1 = s32[128]{0:T(128)S(1)} collective-permute-done((s32[128]{0:T(128)S(1)}, s32[128]{0:T(128)S(1)}, u32[]{:S(2)}, u32[]{:S(2)}) %collective-permute-start.1) | collective-permute-done | bytes 544 | tf_op jit(solution)/shard_map/while/body/eval_jaxpr/ppermute | solution.py:14
  92.5 6.3 %fusion.23 = f32[128,1024]{1,0:T(8,128)S(1)} fusion(bf16[128,4096]{1,0:T(8,128)(2,1)S(1)} %copy.31, bf16[1024,4096]{1,0:T(8,128)(2,1)} %get-tuple-element.114), kind=kOutput, calls=%fused_computation.16.clone.1 | convolution fusion | flops 1073741824 | bytes 9961472 | tf_op jit(solution)/shard_map/while/body/eval_jaxpr/qf,tf->qt/dot_general | solution.py:38
  98.8 5.1 %scatter_fusion = f32[1024,1024]{1,0:T(8,128)} fusion(f32[1024,1024]{1,0:T(8,128)} %get-tuple-element.105, s32[128]{0:T(128)S(1)} %compare_select_fusion.3, f32[128,1024]{1,0:T(8,128)S(1)} %fusion.23), kind=kCustom, calls=%fused_computation.clone.1 | custom fusion | bytes 1573376 | tf_op jit(solution)/shard_map/while/body/eval_jaxpr/scatter | solution.py:41
  103.9 12.5 %collective-permute-done.1 = s32[128]{0:T(128)S(1)} collective-permute-done((s32[128]{0:T(128)S(1)}, s32[128]{0:T(128)S(1)}, u32[]{:S(2)}, u32[]{:S(2)}) %collective-permute-start.1) | collective-permute-done | bytes 544 | tf_op jit(solution)/shard_map/while/body/eval_jaxpr/ppermute | solution.py:14
  116.7 6.3 %fusion.23 = f32[128,1024]{1,0:T(8,128)S(1)} fusion(bf16[128,4096]{1,0:T(8,128)(2,1)S(1)} %copy.31, bf16[1024,4096]{1,0:T(8,128)(2,1)} %get-tuple-element.114), kind=kOutput, calls=%fused_computation.16.clone.1 | convolution fusion | flops 1073741824 | bytes 9961472 | tf_op jit(solution)/shard_map/while/body/eval_jaxpr/qf,tf->qt/dot_general | solution.py:38
  123.0 5.1 %scatter_fusion = f32[1024,1024]{1,0:T(8,128)} fusion(f32[1024,1024]{1,0:T(8,128)} %get-tuple-element.105, s32[128]{0:T(128)S(1)} %compare_select_fusion.3, f32[128,1024]{1,0:T(8,128)S(1)} %fusion.23), kind=kCustom, calls=%fused_computation.clone.1 | custom fusion | bytes 1573376 | tf_op jit(solution)/shard_map/while/body/eval_jaxpr/scatter | solution.py:41
  128.0 11.5 %collective-permute-done.1 = s32[128]{0:T(128)S(1)} collective-permute-done((s32[128]{0:T(128)S(1)}, s32[128]{0:T(128)S(1)}, u32[]{:S(2)}, u32[]{:S(2)}) %collective-permute-start.1) | collective-permute-done | bytes 544 | tf_op jit(solution)/shard_map/while/body/eval_jaxpr/ppermute | solution.py:14
  140.8 6.3 %fusion.23 = f32[128,1024]{1,0:T(8,128)S(1)} fusion(bf16[128,4096]{1,0:T(8,128)(2,1)S(1)} %copy.31, bf16[1024,4096]{1,0:T(8,128)(2,1)} %get-tuple-element.114), kind=kOutput, calls=%fused_computation.16.clone.1 | convolution fusion | flops 1073741824 | bytes 9961472 | tf_op jit(solution)/shard_map/while/body/eval_jaxpr/qf,tf->qt/dot_general | solution.py:38
  147.1 5.1 %scatter_fusion = f32[1024,1024]{1,0:T(8,128)} fusion(f32[1024,1024]{1,0:T(8,128)} %get-tuple-element.105, s32[128]{0:T(128)S(1)} %compare_select_fusion.3, f32[128,1024]{1,0:T(8,128)S(1)} %fusion.23), kind=kCustom, calls=%fused_computation.clone.1 | custom fusion | bytes 1573376 | tf_op jit(solution)/shard_map/while/body/eval_jaxpr/scatter | solution.py:41
  152.2 9.6 %collective-permute-done.1 = s32[128]{0:T(128)S(1)} collective-permute-done((s32[128]{0:T(128)S(1)}, s32[128]{0:T(128)S(1)}, u32[]{:S(2)}, u32[]{:S(2)}) %collective-permute-start.1) | collective-permute-done | bytes 544 | tf_op jit(solution)/shard_map/while/body/eval_jaxpr/ppermute | solution.py:14
  162.0 2.8 collective-permute-start.1
  164.7 6.3 %fusion.23 = f32[128,1024]{1,0:T(8,128)S(1)} fusion(bf16[128,4096]{1,0:T(8,128)(2,1)S(1)} %copy.31, bf16[1024,4096]{1,0:T(8,128)(2,1)} %get-tuple-element.114), kind=kOutput, calls=%fused_computation.16.clone.1 | convolution fusion | flops 1073741824 | bytes 9961472 | tf_op jit(solution)/shard_map/while/body/eval_jaxpr/qf,tf->qt/dot_general | solution.py:38
  171.0 5.1 %scatter_fusion = f32[1024,1024]{1,0:T(8,128)} fusion(f32[1024,1024]{1,0:T(8,128)} %get-tuple-element.105, s32[128]{0:T(128)S(1)} %compare_select_fusion.3, f32[128,1024]{1,0:T(8,128)S(1)} %fusion.23), kind=kCustom, calls=%fused_computation.clone.1 | custom fusion | bytes 1573376 | tf_op jit(solution)/shard_map/while/body/eval_jaxpr/scatter | solution.py:41
  176.1 7.3 %collective-permute-done.1 = s32[128]{0:T(128)S(1)} collective-permute-done((s32[128]{0:T(128)S(1)}, s32[128]{0:T(128)S(1)}, u32[]{:S(2)}, u32[]{:S(2)}) %collective-permute-start.1) | collective-permute-done | bytes 544 | tf_op jit(solution)/shard_map/while/body/eval_jaxpr/ppermute | solution.py:14
  183.5 4.2 %collective-permute-start.1 = (s32[128]{0:T(128)S(1)}, s32[128]{0:T(128)S(1)}, u32[]{:S(2)}, u32[]{:S(2)}) collective-permute-start(s32[128]{0:T(128)S(1)} %copy.32), channel_id=1, source_target_pairs={{224,0},{0,32},{32,64},{64,96},{96,128},{128,160},{160,192},{192,2... | collective-permute-start | bytes 1544 | tf_op jit(solution)/shard_map/while/body/eval_jaxpr/ppermute | solution.py:14
  187.7 6.3 %fusion.23 = f32[128,1024]{1,0:T(8,128)S(1)} fusion(bf16[128,4096]{1,0:T(8,128)(2,1)S(1)} %copy.31, bf16[1024,4096]{1,0:T(8,128)(2,1)} %get-tuple-element.114), kind=kOutput, calls=%fused_computation.16.clone.1 | convolution fusion | flops 1073741824 | bytes 9961472 | tf_op jit(solution)/shard_map/while/body/eval_jaxpr/qf,tf->qt/dot_general | solution.py:38
  194.0 5.1 %scatter_fusion = f32[1024,1024]{1,0:T(8,128)} fusion(f32[1024,1024]{1,0:T(8,128)} %get-tuple-element.105, s32[128]{0:T(128)S(1)} %compare_select_fusion.3, f32[128,1024]{1,0:T(8,128)S(1)} %fusion.23), kind=kCustom, calls=%fused_computation.clone.1 | custom fusion | bytes 1573376 | tf_op jit(solution)/shard_map/while/body/eval_jaxpr/scatter | solution.py:41
  199.1 5.8 %collective-permute-done.1 = s32[128]{0:T(128)S(1)} collective-permute-done((s32[128]{0:T(128)S(1)}, s32[128]{0:T(128)S(1)}, u32[]{:S(2)}, u32[]{:S(2)}) %collective-permute-start.1) | collective-permute-done | bytes 544 | tf_op jit(solution)/shard_map/while/body/eval_jaxpr/ppermute | solution.py:14
  204.9 6.3 %fusion.10 = f32[128,1024]{1,0:T(8,128)S(1)} fusion(bf16[128,4096]{1,0:T(8,128)(2,1)S(1)} %get-tuple-element.36, bf16[1024,4096]{1,0:T(8,128)(2,1)} %get-tuple-element.117), kind=kOutput, calls=%fused_computation.17 | convolution fusion | flops 1073741824 | bytes 9961472 | tf_op jit(solution)/shard_map/qf,tf->qt/dot_general | solution.py:38
  211.2 5.1 %scatter_fusion.1 = f32[1024,1024]{1,0:T(8,128)} fusion(f32[1024,1024]{1,0:T(8,128)} %get-tuple-element.34, s32[128]{0:T(128)S(1)} %compare_select_fusion.1, f32[128,1024]{1,0:T(8,128)S(1)} %fusion.10), kind=kCustom, calls=%fused_computation.1 | custom fusion | bytes 1573376 | tf_op jit(solution)/shard_map/scatter | solution.py:41
  216.3 136.6 %reduce-scatter.2.cloned.1.call-done = f32[32,1024]{1,0:T(8,128)} async-done(((f32[1024,1024]{1,0:T(8,128)}), f32[32,1024]{1,0:T(8,128)}) %reduce-scatter.2.cloned.1.call-update) | async-done | bytes 131088 | tf_op jit(solution)/shard_map/reduce_scatter | solution.py:53
  (55 shorter events, 15.4 us)
Async XLA Ops:
  6.5 5.9 %copy-start = (f32[1,64,64]{2,1,0:T(8,128)S(1)}, f32[1,64,64]{2,1,0:T(8,128)}, u32[]{:S(2)}) copy-start(f32[1,64,64]{2,1,0:T(8,128)} %param.11) | copy-start | bytes 49156
  6.5 346.4 %reduce-scatter.2.cloned.1.call-start = ((), (), s32[]{:S(2)}) async-start(), calls=%async_computation.1 | async-start | bytes 4325376 | tf_op jit(solution)/shard_map/reduce_scatter | solution.py:53
  8.9 9.7 %copy-start.1 = (f32[1,64,64]{2,1,0:T(8,128)S(1)}, f32[1,64,64]{2,1,0:T(8,128)}, u32[]{:S(2)}) copy-start(f32[1,64,64]{2,1,0:T(8,128)} %param.12) | copy-start | bytes 49156
  34.9 5.0 %copy-start.2 = (s32[128]{0:T(128)S(1)}, s32[128]{0:T(128)}, u32[]{:S(2)}) copy-start(s32[128]{0:T(128)} %param.9) | copy-start | bytes 1540
  40.1 27.0 %collective-permute-start = (bf16[128,4096]{1,0:T(8,128)(2,1)S(1)}, bf16[128,4096]{1,0:T(8,128)(2,1)S(1)}, u32[]{:S(2)}, u32[]{:S(2)}) collective-permute-start(bf16[128,4096]{1,0:T(8,128)(2,1)S(1)} %copy.31), channel_id=1, source_target_pairs={{224,0},{0,32},{32,64},{64,96},{96,128},{128,160},{160,192},{192,2... | collective-permute-start | bytes 3145736 | tf_op jit(solution)/shard_map/while/body/eval_jaxpr/ppermute | solution.py:14
  42.3 24.8 %collective-permute-start.1 = (s32[128]{0:T(128)S(1)}, s32[128]{0:T(128)S(1)}, u32[]{:S(2)}, u32[]{:S(2)}) collective-permute-start(s32[128]{0:T(128)S(1)} %copy.32), channel_id=1, source_target_pairs={{224,0},{0,32},{32,64},{64,96},{96,128},{128,160},{160,192},{192,2... | collective-permute-start | bytes 1544 | tf_op jit(solution)/shard_map/while/body/eval_jaxpr/ppermute | solution.py:14
  67.2 25.1 %collective-permute-start = (bf16[128,4096]{1,0:T(8,128)(2,1)S(1)}, bf16[128,4096]{1,0:T(8,128)(2,1)S(1)}, u32[]{:S(2)}, u32[]{:S(2)}) collective-permute-start(bf16[128,4096]{1,0:T(8,128)(2,1)S(1)} %copy.31), channel_id=1, source_target_pairs={{224,0},{0,32},{32,64},{64,96},{96,128},{128,160},{160,192},{192,2... | collective-permute-start | bytes 3145736 | tf_op jit(solution)/shard_map/while/body/eval_jaxpr/ppermute | solution.py:14
  67.3 25.0 %collective-permute-start.1 = (s32[128]{0:T(128)S(1)}, s32[128]{0:T(128)S(1)}, u32[]{:S(2)}, u32[]{:S(2)}) collective-permute-start(s32[128]{0:T(128)S(1)} %copy.32), channel_id=1, source_target_pairs={{224,0},{0,32},{32,64},{64,96},{96,128},{128,160},{160,192},{192,2... | collective-permute-start | bytes 1544 | tf_op jit(solution)/shard_map/while/body/eval_jaxpr/ppermute | solution.py:14
  92.3 24.1 %collective-permute-start = (bf16[128,4096]{1,0:T(8,128)(2,1)S(1)}, bf16[128,4096]{1,0:T(8,128)(2,1)S(1)}, u32[]{:S(2)}, u32[]{:S(2)}) collective-permute-start(bf16[128,4096]{1,0:T(8,128)(2,1)S(1)} %copy.31), channel_id=1, source_target_pairs={{224,0},{0,32},{32,64},{64,96},{96,128},{128,160},{160,192},{192,2... | collective-permute-start | bytes 3145736 | tf_op jit(solution)/shard_map/while/body/eval_jaxpr/ppermute | solution.py:14
  92.4 24.0 %collective-permute-start.1 = (s32[128]{0:T(128)S(1)}, s32[128]{0:T(128)S(1)}, u32[]{:S(2)}, u32[]{:S(2)}) collective-permute-start(s32[128]{0:T(128)S(1)} %copy.32), channel_id=1, source_target_pairs={{224,0},{0,32},{32,64},{64,96},{96,128},{128,160},{160,192},{192,2... | collective-permute-start | bytes 1544 | tf_op jit(solution)/shard_map/while/body/eval_jaxpr/ppermute | solution.py:14
  116.5 23.1 %collective-permute-start = (bf16[128,4096]{1,0:T(8,128)(2,1)S(1)}, bf16[128,4096]{1,0:T(8,128)(2,1)S(1)}, u32[]{:S(2)}, u32[]{:S(2)}) collective-permute-start(bf16[128,4096]{1,0:T(8,128)(2,1)S(1)} %copy.31), channel_id=1, source_target_pairs={{224,0},{0,32},{32,64},{64,96},{96,128},{128,160},{160,192},{192,2... | collective-permute-start | bytes 3145736 | tf_op jit(solution)/shard_map/while/body/eval_jaxpr/ppermute | solution.py:14
  116.6 23.0 %collective-permute-start.1 = (s32[128]{0:T(128)S(1)}, s32[128]{0:T(128)S(1)}, u32[]{:S(2)}, u32[]{:S(2)}) collective-permute-start(s32[128]{0:T(128)S(1)} %copy.32), channel_id=1, source_target_pairs={{224,0},{0,32},{32,64},{64,96},{96,128},{128,160},{160,192},{192,2... | collective-permute-start | bytes 1544 | tf_op jit(solution)/shard_map/while/body/eval_jaxpr/ppermute | solution.py:14
  139.7 22.1 %collective-permute-start = (bf16[128,4096]{1,0:T(8,128)(2,1)S(1)}, bf16[128,4096]{1,0:T(8,128)(2,1)S(1)}, u32[]{:S(2)}, u32[]{:S(2)}) collective-permute-start(bf16[128,4096]{1,0:T(8,128)(2,1)S(1)} %copy.31), channel_id=1, source_target_pairs={{224,0},{0,32},{32,64},{64,96},{96,128},{128,160},{160,192},{192,2... | collective-permute-start | bytes 3145736 | tf_op jit(solution)/shard_map/while/body/eval_jaxpr/ppermute | solution.py:14
  139.8 22.0 %collective-permute-start.1 = (s32[128]{0:T(128)S(1)}, s32[128]{0:T(128)S(1)}, u32[]{:S(2)}, u32[]{:S(2)}) collective-permute-start(s32[128]{0:T(128)S(1)} %copy.32), channel_id=1, source_target_pairs={{224,0},{0,32},{32,64},{64,96},{96,128},{128,160},{160,192},{192,2... | collective-permute-start | bytes 1544 | tf_op jit(solution)/shard_map/while/body/eval_jaxpr/ppermute | solution.py:14
  161.9 21.5 %collective-permute-start = (bf16[128,4096]{1,0:T(8,128)(2,1)S(1)}, bf16[128,4096]{1,0:T(8,128)(2,1)S(1)}, u32[]{:S(2)}, u32[]{:S(2)}) collective-permute-start(bf16[128,4096]{1,0:T(8,128)(2,1)S(1)} %copy.31), channel_id=1, source_target_pairs={{224,0},{0,32},{32,64},{64,96},{96,128},{128,160},{160,192},{192,2... | collective-permute-start | bytes 3145736 | tf_op jit(solution)/shard_map/while/body/eval_jaxpr/ppermute | solution.py:14
  162.0 21.4 %collective-permute-start.1 = (s32[128]{0:T(128)S(1)}, s32[128]{0:T(128)S(1)}, u32[]{:S(2)}, u32[]{:S(2)}) collective-permute-start(s32[128]{0:T(128)S(1)} %copy.32), channel_id=1, source_target_pairs={{224,0},{0,32},{32,64},{64,96},{96,128},{128,160},{160,192},{192,2... | collective-permute-start | bytes 1544 | tf_op jit(solution)/shard_map/while/body/eval_jaxpr/ppermute | solution.py:14
  183.4 21.5 %collective-permute-start = (bf16[128,4096]{1,0:T(8,128)(2,1)S(1)}, bf16[128,4096]{1,0:T(8,128)(2,1)S(1)}, u32[]{:S(2)}, u32[]{:S(2)}) collective-permute-start(bf16[128,4096]{1,0:T(8,128)(2,1)S(1)} %copy.31), channel_id=1, source_target_pairs={{224,0},{0,32},{32,64},{64,96},{96,128},{128,160},{160,192},{192,2... | collective-permute-start | bytes 3145736 | tf_op jit(solution)/shard_map/while/body/eval_jaxpr/ppermute | solution.py:14
  183.5 21.4 %collective-permute-start.1 = (s32[128]{0:T(128)S(1)}, s32[128]{0:T(128)S(1)}, u32[]{:S(2)}, u32[]{:S(2)}) collective-permute-start(s32[128]{0:T(128)S(1)} %copy.32), channel_id=1, source_target_pairs={{224,0},{0,32},{32,64},{64,96},{96,128},{128,160},{160,192},{192,2... | collective-permute-start | bytes 1544 | tf_op jit(solution)/shard_map/while/body/eval_jaxpr/ppermute | solution.py:14
Sparse Core Ops, SparseCore 0:
  216.4 136.4 reduce-scatter.1
where the time goes:
time: 365 us; the launch traced here: 361 us
  waiting for transfers between devices  209 us (57%)
  matrix products  70 us (19%)
  local copies, waits for them, and re-layouts  53.9 us (15%)
  between operations  13.5 us (4%)
  starting transfers between devices  12.7 us (3%)
    reduce_scatter x1, waiting for transfers between devices, on_device(): lax.psum_scatter(partial_value, 'layer', scatter_dimension=0, tiled=True)  137 us
    ppermute x14, waiting for transfers between devices, from_behind(): return lax.ppermute(block, axis, route)  71.9 us
    dot_general x8, matrix products, place_tile(): jnp.einsum('qf,tf->qt', query_block, train_feats, preferred_element_type=...  50 us
    scatter x8, local copies, waits for them, and re-layouts, place_tile(): return partial_value.at[block_ids].set(score_tile)  40.6 us
    ppermute x14, starting transfers between devices, from_behind(): return lax.ppermute(block, axis, route)  12.7 us
    dot_general x2, matrix products, precondition(): jnp.einsum('ai,qij,bj->qab', basis_out, scaled, basis_in, precision=lax.P...  10.2 us
    dot_general x2, matrix products, precondition(): jnp.einsum('ai,qab,bj->qij', basis_out, square, basis_in, precision=lax.P...  9.72 us
  transfers between devices with their start and end apart: 15, of which 8 were waited for; matrix products, arithmetic and copies ran while one was open for 22% of the time, Pallas kernels for 0%

commit v1 on v0

v1 whole, which is shorter than its diff:
```python
import functools
import math

import jax
import jax.numpy as jnp
from jax import lax
from jax.experimental import pallas as pl
from jax.experimental.pallas import tpu as pltpu
from jax.sharding import PartitionSpec as P

damping = 0.1
MESH = pl.DeviceIdType.MESH
f32, bf16 = jnp.float32, jnp.bfloat16

SIZES = {"a": (512, 640, 512, 640), "b": (384, 512, 384, 512)}
PIECES = {}
row = 0
for part in "ab":
    for place, size in enumerate(SIZES[part]):
        PIECES[part + str(place)] = (row, row + size)
        row += size
PART = {"a": (0, 2304), "b": (2304, 4096)}
NAMES = list(PIECES)
UP = ("0", "1", "2", "3")
DOWN = ("2", "3", "0", "1")


def split(x):
    high = x.astype(bf16)
    return high, (x - high.astype(f32)).astype(bf16)


def diagonal(block):
    width = block.shape[0]
    four = jnp.concatenate([block] * 4, axis=1)
    four = jnp.concatenate([four] * 4, axis=0)
    rows = lax.broadcasted_iota(jnp.int32, four.shape, 0) // width
    cols = lax.broadcasted_iota(jnp.int32, four.shape, 1) // width
    return jnp.where(rows == cols, four, 0.0)


def apply_basis(matrix, x):
    high, low = split(x)
    both = jnp.dot(matrix, high, preferred_element_type=f32)
    rest = jnp.dot(matrix[:256], low, preferred_element_type=f32)
    return both[:256] + both[256:] + rest


def kernel(
    g_hbm, ids_ref, t_hbm, bo_ref, bi_ref, eig_ref, out_ref,
    g_v, t_v, q, y1, y2, inv, bdm, acc, cx, rs_send, rs_recv, sums, ids, hot, a_send, a_recv,
    load_sem, q_send, q_recv, id_send, id_recv, cx_ssem, cx_rsem, rs_ssem, rs_rsem, a_ssem, a_rsem,
):
    group, layer = lax.axis_index("group"), lax.axis_index("layer")
    xh, y = group // 4, group % 4
    me, core = layer // 2, layer % 2
    up = (xh * 4 + lax.rem(y + 1, 4), layer)
    down = (xh * 4 + lax.rem(y + 3, 4), layer)
    across = ((1 - xh) * 4 + y, layer)
    sibling = (group, me * 2 + 1 - core)

    barrier = pltpu.get_barrier_semaphore()

    def greet_group(k, c):
        pl.semaphore_signal(barrier, inc=1, device_id=(lax.rem(group + k, 8), layer), device_id_type=MESH)
        return c

    def greet_layer(k, c):
        pl.semaphore_signal(barrier, inc=1, device_id=(group, lax.rem(layer + k, 32)), device_id_type=MESH)
        return c

    lax.fori_loop(1, 8, greet_group, 0)
    lax.fori_loop(1, 32, greet_layer, 0)

    load_g = pltpu.make_async_copy(g_hbm, g_v, load_sem.at[0])
    load_t = pltpu.make_async_copy(t_hbm, t_v, load_sem.at[1])
    load_g.start()
    load_t.start()

    bo = diagonal(bo_ref[...])
    bi = diagonal(bi_ref[...])
    for place, matrix in enumerate((bi.T, bo.T, bo, bi)):
        high, low = split(matrix)
        bdm[place, 0:256, :] = high
        bdm[place, 256:512, :] = low
    scale = 1.0 / (eig_ref[...] + damping)
    for j in range(64):
        inv[j * 64 : j * 64 + 64, :] = jnp.broadcast_to(scale[:, j : j + 1], (64, 128))

    load_g.wait()

    def stage_a(u, c):
        base = pl.multiple_of(u * 512, 512)
        left = g_v[:, pl.ds(base, 256)]
        right = g_v[:, pl.ds(base + 256, 256)]
        both = lax.dot_general(
            bdm[0], jnp.concatenate([left, right], axis=0), (((1,), (1,)), ((), ())), preferred_element_type=f32
        )
        r = both[:256] + both[256:]
        y1[pl.ds(base, 256), :] = r[:, :128]
        y1[pl.ds(base + 256, 256), :] = r[:, 128:]
        return c

    def strided(ref, u):
        halves = []
        for h in range(2):
            halves.append(
                jnp.concatenate([ref[pl.ds(u * 8 + h * 4 + s, 64, stride=64), :] for s in range(4)], axis=0)
            )
        return jnp.concatenate(halves, axis=1)

    def stage_bc(u, c):
        base = pl.multiple_of(u * 512, 512)
        r = apply_basis(bdm[1], strided(y1, u))
        r = r * jnp.concatenate([inv[pl.ds(base, 256), :], inv[pl.ds(base + 256, 256), :]], axis=1)
        r = apply_basis(bdm[2], r)
        y2[pl.ds(base, 256), :] = r[:, :128]
        y2[pl.ds(base + 256, 256), :] = r[:, 128:]
        return c

    def stage_d(u, c):
        base = pl.multiple_of(u * 512, 512)
        r = apply_basis(bdm[3], strided(y2, u)).astype(bf16)
        q[0, pl.ds(base, 256), :] = r[:, :128]
        q[0, pl.ds(base + 256, 256), :] = r[:, 128:]
        return c

    lax.fori_loop(0, 8, stage_a, 0)
    lax.fori_loop(0, 8, stage_bc, 0)
    lax.fori_loop(0, 8, stage_d, 0)

    pl.semaphore_wait(barrier, 38)

    sends = []

    def send(src_slot, piece, target, dst_slot):
        lo, hi = PIECES[piece]
        copy = pltpu.make_async_remote_copy(
            src_ref=q.at[src_slot, pl.ds(lo, hi - lo)],
            dst_ref=q.at[dst_slot, pl.ds(lo, hi - lo)],
            send_sem=q_send.at[len(sends)],
            recv_sem=q_recv.at[dst_slot * 8 + NAMES.index(piece)],
            device_id=target,
            device_id_type=MESH,
        )
        copy.start()
        sends.append(copy)

    def arrive(slot, piece):
        lo, hi = PIECES[piece]
        part = q.at[slot, pl.ds(lo, hi - lo)]
        pltpu.make_async_remote_copy(
            src_ref=part, dst_ref=part, send_sem=q_send.at[0], recv_sem=q_recv.at[slot * 8 + NAMES.index(piece)],
            device_id=up, device_id_type=MESH,
        ).wait_recv()

    for n in "0123":
        send(0, "a" + n, across, 4)
    for above, below in zip(UP, DOWN):
        send(0, "b" + above, up, 3)
        send(0, "b" + below, down, 1)
    for n in "0123":
        send(0, "b" + n, across, 4)
    for above, below in zip(UP, DOWN):
        send(0, "a" + above, up, 3)
        send(0, "a" + below, down, 1)

    def id_target(k):
        return (lax.rem(xh + k // 4, 2) * 4 + lax.rem(y + k, 4), layer)

    def id_slot(k):
        return k // 4 * 4 + (4 - k % 4) % 4

    id_copies = []
    for k in range(1, 8):
        copy = pltpu.make_async_remote_copy(
            src_ref=ids_ref, dst_ref=ids.at[id_slot(k)], send_sem=id_send.at[id_slot(k)], recv_sem=id_recv.at[id_slot(k)],
            device_id=id_target(k), device_id_type=MESH,
        )
        copy.start()
        id_copies.append(copy)
    ids[0] = ids_ref[...]

    def multiply(slot, lo, hi, first):
        def tile(i, c):
            rows = pl.ds(pl.multiple_of(i * 512, 512), 512)
            r = jnp.dot(t_v[rows, lo:hi], q[slot, lo:hi, :], preferred_element_type=f32)
            acc[slot, rows, :] = r if first else acc[slot, rows, :] + r
            return c

        lax.fori_loop(0, 2, tile, 0)

    mine = pl.multiple_of(core * 512, 512)
    theirs = pl.multiple_of((1 - core) * 512, 512)

    def exchange(slot):
        return pltpu.make_async_remote_copy(
            src_ref=acc.at[slot, pl.ds(theirs, 512)], dst_ref=cx.at[slot], send_sem=cx_ssem.at[slot],
            recv_sem=cx_rsem.at[slot], device_id=sibling, device_id_type=MESH,
        )

    def scatter(slot):
        exchange(slot).wait_recv()
        rs_send[slot] = (acc[slot, pl.ds(mine, 512), :] + cx[slot]).astype(bf16)

        def one(k, c):
            to = lax.rem(me + k, 16)
            pltpu.make_async_remote_copy(
                src_ref=rs_send.at[slot, pl.ds(pl.multiple_of(to * 32, 32), 32)],
                dst_ref=rs_recv.at[slot, pl.ds(pl.multiple_of((k - 1) * 32, 32), 32)],
                send_sem=rs_ssem.at[slot], recv_sem=rs_rsem.at[slot],
                device_id=(group, to * 2 + core), device_id_type=MESH,
            ).start()
            return c

        lax.fori_loop(1, 16, one, 0)

    def scattered(slot):
        return pltpu.make_async_remote_copy(
            src_ref=rs_recv.at[slot], dst_ref=rs_recv.at[slot], send_sem=rs_ssem.at[slot], recv_sem=rs_rsem.at[slot],
            device_id=up, device_id_type=MESH,
        )

    def collect(slot):
        scattered(slot).wait_recv()
        own = pl.multiple_of(me * 32, 32)
        total = acc[slot, pl.ds(mine + own, 32), :] + cx[slot, pl.ds(own, 32), :]
        for k in range(15):
            total = total + rs_recv[slot, k * 32 : k * 32 + 32, :].astype(f32)
        sums[:, slot * 128 : slot * 128 + 128] = total

    a, b = PART["a"], PART["b"]
    load_t.wait()
    multiply(0, 0, 4096, True)
    exchange(0).start()

    for n, above, below in zip("0123", UP, DOWN):
        arrive(4, "a" + n)
        send(4, "a" + n, up, 7)
        send(4, "a" + n, down, 5)
        arrive(3, "b" + above)
        if above in "01":
            send(3, "b" + above, up, 2)
        send(3, "b" + above, across, 7)
        arrive(1, "b" + below)
        if below in "23":
            send(1, "b" + below, down, 2)
        send(1, "b" + below, across, 5)
        if n == "0":
            scatter(0)
    multiply(4, *a, True)
    multiply(3, *b, True)
    multiply(1, *b, True)
    for n in "0213":
        arrive(2, "b" + n)
        send(2, "b" + n, across, 6)
    multiply(2, *b, True)
    collect(0)
    for n in "0123":
        arrive(4, "b" + n)
    multiply(4, *b, False)
    exchange(4).start()
    for above, below in zip(UP, DOWN):
        arrive(3, "a" + above)
        if above in "01":
            send(3, "a" + above, up, 2)
        arrive(1, "a" + below)
        if below in "23":
            send(1, "a" + below, down, 2)
    multiply(3, *a, False)
    exchange(3).start()
    multiply(1, *a, False)
    exchange(1).start()
    scatter(4)

    for copy in id_copies:
        copy.wait_recv()
    rows = lax.broadcasted_iota(jnp.int32, (256, 128), 0)
    rows = rows // 8 * 32 + rows % 8
    for k in range(4):
        for s in range(8):
            same = rows + 8 * k == ids[s]
            hot[k * 256 : k * 256 + 256, s * 128 : s * 128 + 128] = jnp.where(same, 1.0, 0.0).astype(bf16)

    scatter(3)
    scatter(1)
    for above, below in zip(UP, DOWN):
        arrive(7, "a" + above)
        if above in "01":
            send(7, "a" + above, up, 6)
        arrive(5, "a" + below)
        if below in "23":
            send(5, "a" + below, down, 6)
    for n in "0213":
        arrive(2, "a" + n)
    multiply(2, *a, False)
    exchange(2).start()
    multiply(7, *a, True)
    multiply(5, *a, True)
    scatter(2)
    collect(4)
    collect(3)
    collect(1)
    for above, below in zip(UP, DOWN):
        arrive(7, "b" + above)
        arrive(5, "b" + below)
    multiply(7, *b, False)
    exchange(7).start()
    multiply(5, *b, False)
    exchange(5).start()
    scatter(7)
    scatter(5)
    collect(2)
    for n in "0213":
        arrive(6, "a" + n)
    multiply(6, *a, True)
    for n in "0213":
        arrive(6, "b" + n)
    multiply(6, *b, False)
    exchange(6).start()
    collect(7)
    collect(5)
    scatter(6)
    collect(6)

    high, low = split(sums[...])
    placed = lax.dot_general(
        hot[...], jnp.concatenate([high, low], axis=0), (((1,), (1,)), ((), ())), preferred_element_type=f32
    )
    placed = (placed[:, :32] + placed[:, 32:]) * (1.0 / math.sqrt(131072))
    placed = jnp.concatenate([placed[k * 256 : k * 256 + 256] for k in range(4)], axis=1)
    a_send[...] = placed.reshape(32, 8, 128)

    place = core * 16 + me

    def deal(k, c):
        to = lax.rem(layer + k, 32)
        pltpu.make_async_remote_copy(
            src_ref=a_send.at[to], dst_ref=a_recv.at[place], send_sem=a_ssem.at[0], recv_sem=a_rsem.at[0],
            device_id=(group, to), device_id_type=MESH,
        ).start()
        return c

    lax.fori_loop(1, 32, deal, 0)
    a_recv[place] = a_send[layer]
    dealt = pltpu.make_async_remote_copy(
        src_ref=a_recv.at[pl.ds(0, 31)], dst_ref=a_recv.at[pl.ds(0, 31)], send_sem=a_ssem.at[0], recv_sem=a_rsem.at[0],
        device_id=up, device_id_type=MESH,
    )
    dealt.wait_recv()
    for m in range(8):
        tiles = [a_recv[4 * m + n] for n in range(4)]
        for k in range(4):
            out_ref[8 * k : 8 * k + 8, 128 * m : 128 * m + 128] = jnp.concatenate(
                [tile[:, 32 * k : 32 * k + 32] for tile in tiles], axis=1
            )

    for copy in sends:
        copy.wait_send()
    for copy in id_copies:
        copy.wait_send()
    for slot in range(8):
        exchange(slot).wait_send()
        scattered(slot).wait_send()
    dealt.wait_send()


def on_device(query_grads, query_ids, train_feats, basis_out, basis_in, eigen_vals):
    anywhere = pl.BlockSpec(memory_space=pl.ANY)
    vmem = pl.BlockSpec(memory_space=pltpu.VMEM)
    dma = pltpu.SemaphoreType.DMA
    return pl.pallas_call(
        kernel,
        out_shape=jax.ShapeDtypeStruct((32, 1024), f32),
        in_specs=[anywhere, vmem, anywhere, vmem, vmem, vmem],
        out_specs=vmem,
        scratch_shapes=[
            pltpu.VMEM((128, 4096), bf16),
            pltpu.VMEM((1024, 4096), bf16),
            pltpu.VMEM((8, 4096, 128), bf16),
            pltpu.VMEM((4096, 128), f32),
            pltpu.VMEM((4096, 128), f32),
            pltpu.VMEM((4096, 128), f32),
            pltpu.VMEM((4, 512, 256), bf16),
            pltpu.VMEM((8, 1024, 128), f32),
            pltpu.VMEM((8, 512, 128), f32),
            pltpu.VMEM((8, 512, 128), bf16),
            pltpu.VMEM((8, 480, 128), bf16),
            pltpu.VMEM((32, 1024), f32),
            pltpu.VMEM((8, 1, 128), jnp.int32),
            pltpu.VMEM((1024, 1024), bf16),
            pltpu.VMEM((32, 8, 128), f32),
            pltpu.VMEM((32, 8, 128), f32),
            dma((2,)),
            dma((56,)),
            dma((64,)),
            dma((8,)),
            dma((8,)),
            dma((8,)),
            dma((8,)),
            dma((8,)),
            dma((8,)),
            dma((1,)),
            dma((1,)),
        ],
        compiler_params=pltpu.CompilerParams(
            collective_id=0, has_side_effects=True, vmem_limit_bytes=56 * 2**20
        ),
        name="influence",
    )(
        query_grads,
        query_ids.reshape(1, 128),
        train_feats,
        basis_out[0],
        basis_in[0],
        eigen_vals[0],
    )


def solution(mesh):
    return jax.shard_map(
        on_device,
        mesh=mesh,
        in_specs=(
            P("group", "layer"),
            P("group"),
            P("group", "layer"),
            P("layer", None, None),
            P("layer", None, None),
            P("layer", None, None),
        ),
        out_specs=P("layer", "group"),
        check_vma=False,
    )
```

time: 365 us -> 110 us (0.30); the launches traced: 361 us -> 110 us
  waiting for transfers between devices: 209 us -> 0 us
  Pallas kernels: 0 us -> 109 us
  matrix products: 70 us -> 0 us
  local copies, waits for them, and re-layouts: 53.9 us -> 1.57 us
  between operations: 13.5 us -> 0.01 us
  starting transfers between devices: 12.7 us -> 0 us
    reduce_scatter x1 -> x0, waiting for transfers between devices: 137 us -> none  [on_device(): lax.psum_scatter(partial_value, 'layer', scatter_dimension=0, tiled=True)]
    pallas_call x0 -> x1, Pallas kernels: none -> 109 us  [on_device(): pl.pallas_call(kernel, out_shape=jax.ShapeDtypeStruct((32, 1024), f32), i...]
    ppermute x14 -> x0, waiting for transfers between devices: 71.9 us -> none  [from_behind(): return lax.ppermute(block, axis, route)]
    dot_general x12 -> x0, matrix products: 70 us -> none  [the longest x8 50 us: place_tile(): jnp.einsum('qf,tf->qt', query_block, train_feats, preferred_element_type=...]
    scatter x8 -> x0, local copies, waits for them, and re-layouts: 40.6 us -> none  [place_tile(): return partial_value.at[block_ids].set(score_tile)]
    ppermute x14 -> x0, starting transfers between devices: 12.7 us -> none  [from_behind(): return lax.ppermute(block, axis, route)]
    dot_general x1 -> x0, local copies, waits for them, and re-layouts: 4.51 us -> none  [precondition(): jnp.einsum('ai,qij,bj->qab', basis_out, scaled, basis_in, precision=lax.P...]
  transfers between devices with their start and end apart: 15 -> 0, of which waited for: 8 -> 0; matrix products, arithmetic and copies ran while one was open for 22% -> 0% of each run, Pallas kernels for 0% -> 0%
where the time goes in v1:
time: 110 us
  Pallas kernels  109 us (99%)
  local copies, waits for them, and re-layouts  1.57 us (1%)
    pallas_call x1, Pallas kernels, on_device(): pl.pallas_call(kernel, out_shape=jax.ShapeDtypeStruct((32, 1024), f32), i...  109 us

profile of v1, /device:TPU:1, one launch (start us, length us, event | category | flops | bytes accessed | tf_op | source)
XLA Modules:
  0.0 110.3 jit_solution(5793372519642831367)
XLA Ops:
  0.0 108.7 %influence.1 = f32[32,1024]{1,0:T(8,128)} custom-call(bf16[128,4096]{1,0:T(8,128)(2,1)} %g_hbm.1, s32[1,128]{1,0:T(1,128)} %bitcast.7, bf16[1024,4096]{1,0:T(8,128)(2,1)} %t_hbm.1, f32[64,64]{1,0:T(8,128)} %bitcast.4, f32[64,64]{1,0:T(8,128)} %bitcast.5, f32[64,64]{1,0:T(8,128)} %bitcast.6), custom_call_target="tpu_custom_call" | custom-call | tf_op jit(solution)/shard_map/influence/pallas_call | solution.py:372
  108.7 1.6 %copy.8 = f32[32,1024]{1,0:T(8,128)} copy(f32[32,1024]{1,0:T(8,128)} %influence.1) | data formatting | bytes 262144

commit v2 on v1

--- a/solution.py
+++ b/solution.py
@@ -22,6 +22,7 @@
 PART = {"a": (0, 2304), "b": (2304, 4096)}
 NAMES = list(PIECES)
 UP = ("0", "1", "2", "3")
+LAST = 6
 DOWN = ("2", "3", "0", "1")
 
 
@@ -39,6 +40,10 @@
     return jnp.where(rows == cols, four, 0.0)
 
 
+def far(n, count):
+    return count // 2 + (n % 2 * 2 - 1) * ((n + 1) // 2)
+
+
 def apply_basis(matrix, x):
     high, low = split(x)
     both = jnp.dot(matrix, high, preferred_element_type=f32)
@@ -48,12 +53,13 @@
 
 def kernel(
     g_hbm, ids_ref, t_hbm, bo_ref, bi_ref, eig_ref, out_ref,
-    g_v, t_v, q, y1, y2, inv, bdm, acc, cx, rs_send, rs_recv, sums, ids, hot, a_send, a_recv,
-    load_sem, q_send, q_recv, id_send, id_recv, cx_ssem, cx_rsem, rs_ssem, rs_rsem, a_ssem, a_rsem,
+    g_v, t_v, q, y1, y2, inv, bdm, acc, cx, rs_send, rs_recv, zs, xs, ids, hot, a_send, a_recv,
+    load_sem, q_send, q_recv, id_send, id_recv, cx_ssem, cx_rsem, rs_ssem, rs_rsem, xs_ssem, xs_rsem, a_ssem, a_rsem,
 ):
     group, layer = lax.axis_index("group"), lax.axis_index("layer")
     xh, y = group // 4, group % 4
     me, core = layer // 2, layer % 2
+    z, xl = me // 2, me % 2
     up = (xh * 4 + lax.rem(y + 1, 4), layer)
     down = (xh * 4 + lax.rem(y + 3, 4), layer)
     across = ((1 - xh) * 4 + y, layer)
@@ -125,9 +131,9 @@
         q[0, pl.ds(base + 256, 256), :] = r[:, 128:]
         return c
 
-    lax.fori_loop(0, 8, stage_a, 0)
-    lax.fori_loop(0, 8, stage_bc, 0)
-    lax.fori_loop(0, 8, stage_d, 0)
+    lax.fori_loop(0, 8, stage_a, 0, unroll=8)
+    lax.fori_loop(0, 8, stage_bc, 0, unroll=8)
+    lax.fori_loop(0, 8, stage_d, 0, unroll=8)
 
     pl.semaphore_wait(barrier, 38)
 
@@ -161,9 +167,6 @@
         send(0, "b" + below, down, 1)
     for n in "0123":
         send(0, "b" + n, across, 4)
-    for above, below in zip(UP, DOWN):
-        send(0, "a" + above, up, 3)
-        send(0, "a" + below, down, 1)
 
     def id_target(k):
         return (lax.rem(xh + k // 4, 2) * 4 + lax.rem(y + k, 4), layer)
@@ -202,146 +205,205 @@
     def scatter(slot):
         exchange(slot).wait_recv()
         rs_send[slot] = (acc[slot, pl.ds(mine, 512), :] + cx[slot]).astype(bf16)
-
-        def one(k, c):
-            to = lax.rem(me + k, 16)
+        count, size = (16, 32) if slot == LAST else (8, 64)
+        here = me if slot == LAST else z
+
+        def one(n, c):
+            k = far(n, count)
+            to = lax.rem(here + k, count)
+            target = to * 2 + core if slot == LAST else to * 4 + xl * 2 + core
             pltpu.make_async_remote_copy(
-                src_ref=rs_send.at[slot, pl.ds(pl.multiple_of(to * 32, 32), 32)],
-                dst_ref=rs_recv.at[slot, pl.ds(pl.multiple_of((k - 1) * 32, 32), 32)],
+                src_ref=rs_send.at[slot, pl.ds(pl.multiple_of(to * size, size), size)],
+                dst_ref=rs_recv.at[slot, pl.ds(pl.multiple_of((k - 1) * size, size), size)],
                 send_sem=rs_ssem.at[slot], recv_sem=rs_rsem.at[slot],
-                device_id=(group, to * 2 + core), device_id_type=MESH,
+                device_id=(group, target), device_id_type=MESH,
             ).start()
             return c
 
-        lax.fori_loop(1, 16, one, 0)
+        lax.fori_loop(0, count - 1, one, 0)
 
     def scattered(slot):
+        landed = rs_recv.at[slot, pl.ds(0, 480 if slot == LAST else 448)]
         return pltpu.make_async_remote_copy(
-            src_ref=rs_recv.at[slot], dst_ref=rs_recv.at[slot], send_sem=rs_ssem.at[slot], recv_sem=rs_rsem.at[slot],
+            src_ref=landed, dst_ref=landed, send_sem=rs_ssem.at[slot], recv_sem=rs_rsem.at[slot],
             device_id=up, device_id_type=MESH,
         )
 
+    def summed(slot, size):
+        scattered(slot).wait_recv()
+        own = pl.multiple_of((me if slot == LAST else z) * size, size)
+        total = acc[slot, pl.ds(mine + own, size), :] + cx[slot, pl.ds(own, size), :]
+        for k in range(512 // size - 1):
+            total = total + rs_recv[slot, k * size : k * size + size, :].astype(f32)
+        return total
+
+    def swap(slot):
+        return pltpu.make_async_remote_copy(
+            src_ref=zs.at[slot, pl.ds(pl.multiple_of((1 - xl) * 32, 32), 32)], dst_ref=xs.at[slot],
+            send_sem=xs_ssem.at[slot], recv_sem=xs_rsem.at[slot],
+            device_id=(group, z * 4 + (1 - xl) * 2 + core), device_id_type=MESH,
+        )
+
+    def zsum(slot):
+        zs[slot] = summed(slot, 64)
+        swap(slot).start()
+
     def collect(slot):
-        scattered(slot).wait_recv()
-        own = pl.multiple_of(me * 32, 32)
-        total = acc[slot, pl.ds(mine + own, 32), :] + cx[slot, pl.ds(own, 32), :]
-        for k in range(15):
-            total = total + rs_recv[slot, k * 32 : k * 32 + 32, :].astype(f32)
-        sums[:, slot * 128 : slot * 128 + 128] = total
+        if slot == LAST:
+            total = summed(slot, 32)
+        else:
+            swap(slot).wait_recv()
+            total = zs[slot, pl.ds(pl.multiple_of(xl * 32, 32), 32), :] + xs[slot]
+        placed = None
+        for half in split(total):
+            none = jnp.zeros_like(half)
+            spread = jnp.concatenate(
+                [jnp.concatenate([half if m == k else none for m in range(4)], axis=1) for k in range(4)], axis=0
+            )
+            term = lax.dot_general(hot[slot], spread, (((1,), (1,)), ((), ())), preferred_element_type=f32)
+            placed = term if placed is None else placed + term
+        placed = placed.reshape(32, 8, 128)
+        a_send[...] = placed if slot == 0 else a_send[...] + placed
+
+    def piece(slot, name, first):
+        arrive(slot, name)
+        multiply(slot, *PIECES[name], first)
 
     a, b = PART["a"], PART["b"]
     load_t.wait()
     multiply(0, 0, 4096, True)
     exchange(0).start()
 
-    for n, above, below in zip("0123", UP, DOWN):
+    def neighbours_b(above, below):
+        arrive(3, "b" + above)
+        arrive(1, "b" + below)
+        if above in "01":
+            send(3, "b" + above, up, 2)
+            send(1, "b" + below, down, 2)
+        send(3, "b" + above, across, 7)
+        send(1, "b" + below, across, 5)
+
+    def partner_a(n):
         arrive(4, "a" + n)
         send(4, "a" + n, up, 7)
         send(4, "a" + n, down, 5)
-        arrive(3, "b" + above)
+
+    def neighbours_a(above, below):
+        arrive(3, "a" + above)
+        arrive(1, "a" + below)
         if above in "01":
-            send(3, "b" + above, up, 2)
-        send(3, "b" + above, across, 7)
-        arrive(1, "b" + below)
-        if below in "23":
-            send(1, "b" + below, down, 2)
-        send(1, "b" + below, across, 5)
-        if n == "0":
-            scatter(0)
+            send(3, "a" + above, up, 2)
+            send(1, "a" + below, down, 2)
+
+    def second_a(above, below):
+        arrive(7, "a" + above)
+        arrive(5, "a" + below)
+        if above in "01":
+            send(7, "a" + above, up, 6)
+            send(5, "a" + below, down, 6)
+
+    neighbours_b("0", "2")
+    neighbours_b("1", "3")
+    for above, below in zip(UP, DOWN):
+        send(0, "a" + above, up, 3)
+        send(0, "a" + below, down, 1)
+    partner_a("0")
+    scatter(0)
+    partner_a("1")
+    neighbours_b("2", "0")
+    neighbours_b("3", "1")
+    partner_a("2")
+
+    for copy in id_copies:
+        copy.wait_recv()
+    rows = lax.broadcasted_iota(jnp.int32, (256, 128), 0)
+    rows = rows // 8 * 32 + rows % 8
+    for s in range(8):
+        for k in range(4):
+            same = rows + 8 * k == ids[s]
+            hot[s, :, k * 128 : k * 128 + 128] = jnp.where(same, 1.0, 0.0).astype(bf16)
+
+    partner_a("3")
     multiply(4, *a, True)
-    multiply(3, *b, True)
-    multiply(1, *b, True)
     for n in "0213":
         arrive(2, "b" + n)
         send(2, "b" + n, across, 6)
+    multiply(3, *b, True)
+    multiply(1, *b, True)
+    neighbours_a("0", "2")
     multiply(2, *b, True)
-    collect(0)
+    neighbours_a("1", "3")
     for n in "0123":
         arrive(4, "b" + n)
     multiply(4, *b, False)
     exchange(4).start()
-    for above, below in zip(UP, DOWN):
-        arrive(3, "a" + above)
-        if above in "01":
-            send(3, "a" + above, up, 2)
-        arrive(1, "a" + below)
-        if below in "23":
-            send(1, "a" + below, down, 2)
+    zsum(0)
+    neighbours_a("2", "0")
+    scatter(4)
+    neighbours_a("3", "1")
     multiply(3, *a, False)
     exchange(3).start()
     multiply(1, *a, False)
     exchange(1).start()
-    scatter(4)
-
-    for copy in id_copies:
-        copy.wait_recv()
-    rows = lax.broadcasted_iota(jnp.int32, (256, 128), 0)
-    rows = rows // 8 * 32 + rows % 8
-    for k in range(4):
-        for s in range(8):
-            same = rows + 8 * k == ids[s]
-            hot[k * 256 : k * 256 + 256, s * 128 : s * 128 + 128] = jnp.where(same, 1.0, 0.0).astype(bf16)
-
+    second_a("0", "2")
     scatter(3)
+    second_a("1", "3")
     scatter(1)
-    for above, below in zip(UP, DOWN):
-        arrive(7, "a" + above)
-        if above in "01":
-            send(7, "a" + above, up, 6)
-        arrive(5, "a" + below)
-        if below in "23":
-            send(5, "a" + below, down, 6)
+    zsum(4)
+    second_a("2", "0")
+    second_a("3", "1")
+    multiply(7, *a, True)
+    multiply(5, *a, True)
+    zsum(3)
+    for n in "0123":
+        arrive(7, "b" + n)
+    multiply(7, *b, False)
+    exchange(7).start()
+    for n in "0123":
+        arrive(5, "b" + n)
+    multiply(5, *b, False)
+    exchange(5).start()
+    zsum(1)
     for n in "0213":
         arrive(2, "a" + n)
+    scatter(7)
     multiply(2, *a, False)
     exchange(2).start()
-    multiply(7, *a, True)
-    multiply(5, *a, True)
+    scatter(5)
+    collect(0)
+    piece(6, "b0", True)
+    piece(6, "b2", False)
     scatter(2)
+    piece(6, "a0", False)
+    piece(6, "a2", False)
+    piece(6, "b1", False)
+    zsum(7)
+    piece(6, "b3", False)
+    piece(6, "a1", False)
+    piece(6, "a3", False)
+    exchange(6).start()
+    zsum(5)
     collect(4)
+    scatter(6)
+    zsum(2)
     collect(3)
     collect(1)
-    for above, below in zip(UP, DOWN):
-        arrive(7, "b" + above)
-        arrive(5, "b" + below)
-    multiply(7, *b, False)
-    exchange(7).start()
-    multiply(5, *b, False)
-    exchange(5).start()
-    scatter(7)
-    scatter(5)
-    collect(2)
-    for n in "0213":
-        arrive(6, "a" + n)
-    multiply(6, *a, True)
-    for n in "0213":
-        arrive(6, "b" + n)
-    multiply(6, *b, False)
-    exchange(6).start()
     collect(7)
     collect(5)
-    scatter(6)
+    collect(2)
     collect(6)
 
-    high, low = split(sums[...])
-    placed = lax.dot_general(
-        hot[...], jnp.concatenate([high, low], axis=0), (((1,), (1,)), ((), ())), preferred_element_type=f32
-    )
-    placed = (placed[:, :32] + placed[:, 32:]) * (1.0 / math.sqrt(131072))
-    placed = jnp.concatenate([placed[k * 256 : k * 256 + 256] for k in range(4)], axis=1)
-    a_send[...] = placed.reshape(32, 8, 128)
-
     place = core * 16 + me
 
-    def deal(k, c):
-        to = lax.rem(layer + k, 32)
+    def deal(n, c):
+        to = lax.rem(layer + far(n, 32), 32)
         pltpu.make_async_remote_copy(
             src_ref=a_send.at[to], dst_ref=a_recv.at[place], send_sem=a_ssem.at[0], recv_sem=a_rsem.at[0],
             device_id=(group, to), device_id_type=MESH,
         ).start()
         return c
 
-    lax.fori_loop(1, 32, deal, 0)
+    lax.fori_loop(0, 31, deal, 0)
     a_recv[place] = a_send[layer]
     dealt = pltpu.make_async_remote_copy(
         src_ref=a_recv.at[pl.ds(0, 31)], dst_ref=a_recv.at[pl.ds(0, 31)], send_sem=a_ssem.at[0], recv_sem=a_rsem.at[0],
@@ -362,6 +424,8 @@
     for slot in range(8):
         exchange(slot).wait_send()
         scattered(slot).wait_send()
+        if slot != LAST:
+            swap(slot).wait_send()
     dealt.wait_send()
 
 
@@ -386,14 +450,17 @@
             pltpu.VMEM((8, 512, 128), f32),
             pltpu.VMEM((8, 512, 128), bf16),
             pltpu.VMEM((8, 480, 128), bf16),
-            pltpu.VMEM((32, 1024), f32),
+            pltpu.VMEM((8, 64, 128), f32),
+            pltpu.VMEM((8, 32, 128), f32),
             pltpu.VMEM((8, 1, 128), jnp.int32),
-            pltpu.VMEM((1024, 1024), bf16),
+            pltpu.VMEM((8, 256, 512), bf16),
             pltpu.VMEM((32, 8, 128), f32),
             pltpu.VMEM((32, 8, 128), f32),
             dma((2,)),
             dma((56,)),
             dma((64,)),
+            dma((8,)),
+            dma((8,)),
             dma((8,)),
             dma((8,)),
             dma((8,)),
@@ -414,7 +481,7 @@
         basis_out[0],
         basis_in[0],
         eigen_vals[0],
-    )
+    ) * (1.0 / math.sqrt(131072))
 
 
 def solution(mesh):

time: 110 us -> 89.8 us (0.82)
  Pallas kernels: 109 us -> 88 us
  other arithmetic: 0 us -> 1.57 us
  local copies, waits for them, and re-layouts: 1.57 us -> 0 us
    pallas_call x1, Pallas kernels: 109 us -> 88 us  [on_device(): pl.pallas_call(kernel, out_shape=jax.ShapeDtypeStruct((32, 1024), f32), i...]
    mul x0 -> x1, other arithmetic: none -> 1.57 us  [on_device(): pl.pallas_call(kernel, out_shape=jax.ShapeDtypeStruct((32, 1024), f32), i...]
    unnamed x1 -> x0, local copies, waits for them, and re-layouts: 1.57 us -> none
where the time goes in v2:
time: 89.8 us; the launch traced here: 89.6 us
  Pallas kernels  88 us (98%)
  other arithmetic  1.57 us (2%)
    pallas_call x1, Pallas kernels, on_device(): pl.pallas_call(kernel, out_shape=jax.ShapeDtypeStruct((32, 1024), f32), i...  88 us

profile of v2, /device:TPU:1, one launch (start us, length us, event | category | flops | bytes accessed | tf_op | source)
XLA Modules:
  0.0 89.6 jit_solution(1722618039554088975)
XLA Ops:
  0.0 88.0 %influence.1 = f32[32,1024]{1,0:T(8,128)} custom-call(bf16[128,4096]{1,0:T(8,128)(2,1)} %g_hbm.1, s32[1,128]{1,0:T(1,128)} %bitcast.7, bf16[1024,4096]{1,0:T(8,128)(2,1)} %t_hbm.1, f32[64,64]{1,0:T(8,128)} %bitcast.4, f32[64,64]{1,0:T(8,128)} %bitcast.5, f32[64,64]{1,0:T(8,128)} %bitcast.6), custom_call_target="tpu_custom_call" | custom-call | tf_op jit(solution)/shard_map/influence/pallas_call | solution.py:436
  88.0 1.6 %broadcast_multiply_fusion = f32[32,1024]{1,0:T(8,128)} fusion(f32[32,1024]{1,0:T(8,128)} %influence.1), kind=kLoop, calls=%fused_computation | loop fusion | flops 32768 | bytes 262144 | tf_op jit(solution)/shard_map/mul | solution.py:436

commit v3 on v2

--- a/solution.py
+++ b/solution.py
@@ -12,15 +12,17 @@
 MESH = pl.DeviceIdType.MESH
 f32, bf16 = jnp.float32, jnp.bfloat16
 
-SIZES = {"a": (512, 640, 512, 640), "b": (384, 512, 384, 512)}
+ORDER = (
+    ("a0", 512), ("b0", 384), ("b2", 384), ("a1", 640), ("a2", 512), ("b1", 512), ("b3", 512), ("a3", 640),
+)
 PIECES = {}
 row = 0
-for part in "ab":
-    for place, size in enumerate(SIZES[part]):
-        PIECES[part + str(place)] = (row, row + size)
-        row += size
-PART = {"a": (0, 2304), "b": (2304, 4096)}
+for name, size in ORDER:
+    PIECES[name] = (row, row + size)
+    row += size
 NAMES = list(PIECES)
+A = ((0, 512), (1280, 2432), (3456, 4096))
+B = ((512, 1280), (2432, 3456))
 UP = ("0", "1", "2", "3")
 LAST = 6
 DOWN = ("2", "3", "0", "1")
@@ -65,6 +67,10 @@
     across = ((1 - xh) * 4 + y, layer)
     sibling = (group, me * 2 + 1 - core)
 
+    load_g = pltpu.make_async_copy(g_hbm, g_v, load_sem.at[0])
+    load_t = pltpu.make_async_copy(t_hbm, t_v, load_sem.at[1])
+    load_g.start()
+
     barrier = pltpu.get_barrier_semaphore()
 
     def greet_group(k, c):
@@ -75,12 +81,8 @@
         pl.semaphore_signal(barrier, inc=1, device_id=(group, lax.rem(layer + k, 32)), device_id_type=MESH)
         return c
 
-    lax.fori_loop(1, 8, greet_group, 0)
-    lax.fori_loop(1, 32, greet_layer, 0)
-
-    load_g = pltpu.make_async_copy(g_hbm, g_v, load_sem.at[0])
-    load_t = pltpu.make_async_copy(t_hbm, t_v, load_sem.at[1])
-    load_g.start()
+    lax.fori_loop(1, 8, greet_group, 0, unroll=7)
+    lax.fori_loop(1, 32, greet_layer, 0, unroll=31)
     load_t.start()
 
     bo = diagonal(bo_ref[...])
@@ -133,7 +135,7 @@
 
     lax.fori_loop(0, 8, stage_a, 0, unroll=8)
     lax.fori_loop(0, 8, stage_bc, 0, unroll=8)
-    lax.fori_loop(0, 8, stage_d, 0, unroll=8)
+    lax.fori_loop(0, 3, stage_d, 0, unroll=3)
 
     pl.semaphore_wait(barrier, 38)
 
@@ -160,9 +162,13 @@
             device_id=up, device_id_type=MESH,
         ).wait_recv()
 
-    for n in "0123":
+    send(0, "a0", across, 4)
+    send(0, "b0", up, 3)
+    send(0, "b2", down, 1)
+    lax.fori_loop(3, 8, stage_d, 0, unroll=5)
+    for n in "123":
         send(0, "a" + n, across, 4)
-    for above, below in zip(UP, DOWN):
+    for above, below in zip(UP[1:], DOWN[1:]):
         send(0, "b" + above, up, 3)
         send(0, "b" + below, down, 1)
     for n in "0123":
@@ -184,17 +190,22 @@
         id_copies.append(copy)
     ids[0] = ids_ref[...]
 
-    def multiply(slot, lo, hi, first):
-        def tile(i, c):
-            rows = pl.ds(pl.multiple_of(i * 512, 512), 512)
-            r = jnp.dot(t_v[rows, lo:hi], q[slot, lo:hi, :], preferred_element_type=f32)
-            acc[slot, rows, :] = r if first else acc[slot, rows, :] + r
-            return c
-
-        lax.fori_loop(0, 2, tile, 0)
-
     mine = pl.multiple_of(core * 512, 512)
     theirs = pl.multiple_of((1 - core) * 512, 512)
+
+    def half(slot, ranges, first, start):
+        r = None if first else acc[slot, pl.ds(start, 512), :]
+        for lo, hi in ranges:
+            term = jnp.dot(t_v[pl.ds(start, 512), lo:hi], q[slot, lo:hi, :], preferred_element_type=f32)
+            r = term if r is None else r + term
+        acc[slot, pl.ds(start, 512), :] = r
+
+    def multiply(slot, ranges, first):
+        def tile(i, c):
+            half(slot, ranges, first, pl.multiple_of(i * 512, 512))
+            return c
+
+        lax.fori_loop(0, 2, tile, 0)
 
     def exchange(slot):
         return pltpu.make_async_remote_copy(
@@ -220,7 +231,7 @@
             ).start()
             return c
 
-        lax.fori_loop(0, count - 1, one, 0)
+        lax.fori_loop(0, count - 1, one, 0, unroll=count - 1)
 
     def scattered(slot):
         landed = rs_recv.at[slot, pl.ds(0, 480 if slot == LAST else 448)]
@@ -246,7 +257,6 @@
 
     def zsum(slot):
         zs[slot] = summed(slot, 64)
-        swap(slot).start()
 
     def collect(slot):
         if slot == LAST:
@@ -267,11 +277,10 @@
 
     def piece(slot, name, first):
         arrive(slot, name)
-        multiply(slot, *PIECES[name], first)
-
-    a, b = PART["a"], PART["b"]
+        multiply(slot, (PIECES[name],), first)
+
     load_t.wait()
-    multiply(0, 0, 4096, True)
+    multiply(0, ((0, 4096),), True)
     exchange(0).start()
 
     def neighbours_b(above, below):
@@ -324,26 +333,26 @@
             hot[s, :, k * 128 : k * 128 + 128] = jnp.where(same, 1.0, 0.0).astype(bf16)
 
     partner_a("3")
-    multiply(4, *a, True)
+    multiply(4, A, True)
     for n in "0213":
         arrive(2, "b" + n)
         send(2, "b" + n, across, 6)
-    multiply(3, *b, True)
-    multiply(1, *b, True)
+    multiply(3, B, True)
+    multiply(1, B, True)
     neighbours_a("0", "2")
-    multiply(2, *b, True)
+    multiply(2, B, True)
     neighbours_a("1", "3")
     for n in "0123":
         arrive(4, "b" + n)
-    multiply(4, *b, False)
+    multiply(4, B, False)
     exchange(4).start()
     zsum(0)
     neighbours_a("2", "0")
     scatter(4)
     neighbours_a("3", "1")
-    multiply(3, *a, False)
+    multiply(3, A, False)
     exchange(3).start()
-    multiply(1, *a, False)
+    multiply(1, A, False)
     exchange(1).start()
     second_a("0", "2")
     scatter(3)
@@ -352,40 +361,47 @@
     zsum(4)
     second_a("2", "0")
     second_a("3", "1")
-    multiply(7, *a, True)
-    multiply(5, *a, True)
+    multiply(7, A, True)
+    multiply(5, A, True)
     zsum(3)
     for n in "0123":
         arrive(7, "b" + n)
-    multiply(7, *b, False)
+    multiply(7, B, False)
     exchange(7).start()
     for n in "0123":
         arrive(5, "b" + n)
-    multiply(5, *b, False)
+    multiply(5, B, False)
     exchange(5).start()
     zsum(1)
     for n in "0213":
         arrive(2, "a" + n)
     scatter(7)
-    multiply(2, *a, False)
+    multiply(2, A, False)
     exchange(2).start()
     scatter(5)
-    collect(0)
+    for slot in (0, 4, 3, 1):
+        swap(slot).start()
     piece(6, "b0", True)
     piece(6, "b2", False)
     scatter(2)
     piece(6, "a0", False)
     piece(6, "a2", False)
     piece(6, "b1", False)
-    zsum(7)
     piece(6, "b3", False)
     piece(6, "a1", False)
-    piece(6, "a3", False)
+    arrive(6, "a3")
+    half(6, (PIECES["a3"],), False, theirs)
     exchange(6).start()
+    half(6, (PIECES["a3"],), False, mine)
+    zsum(7)
+    swap(7).start()
+    collect(0)
+    scatter(6)
     zsum(5)
+    swap(5).start()
+    zsum(2)
+    swap(2).start()
     collect(4)
-    scatter(6)
-    zsum(2)
     collect(3)
     collect(1)
     collect(7)
@@ -403,7 +419,7 @@
         ).start()
         return c
 
-    lax.fori_loop(0, 31, deal, 0)
+    lax.fori_loop(0, 31, deal, 0, unroll=31)
     a_recv[place] = a_send[layer]
     dealt = pltpu.make_async_remote_copy(
         src_ref=a_recv.at[pl.ds(0, 31)], dst_ref=a_recv.at[pl.ds(0, 31)], send_sem=a_ssem.at[0], recv_sem=a_rsem.at[0],

time: 89.8 us -> 86.4 us (0.962)
  Pallas kernels: 88 us -> 84.7 us
    pallas_call x1, Pallas kernels: 88 us -> 84.7 us  [on_device(): pl.pallas_call(kernel, out_shape=jax.ShapeDtypeStruct((32, 1024), f32), i...]
where the time goes in v3:
time: 86.4 us; the launch traced here: 86.3 us
  Pallas kernels  84.7 us (98%)
  other arithmetic  1.57 us (2%)
    pallas_call x1, Pallas kernels, on_device(): pl.pallas_call(kernel, out_shape=jax.ShapeDtypeStruct((32, 1024), f32), i...  84.7 us

profile of v3, /device:TPU:1, one launch (start us, length us, event | category | flops | bytes accessed | tf_op | source)
XLA Modules:
  0.0 86.3 jit_solution(1013251209817710362)
XLA Ops:
  0.0 84.7 %influence.1 = f32[32,1024]{1,0:T(8,128)} custom-call(bf16[128,4096]{1,0:T(8,128)(2,1)} %g_hbm.1, s32[1,128]{1,0:T(1,128)} %bitcast.7, bf16[1024,4096]{1,0:T(8,128)(2,1)} %t_hbm.1, f32[64,64]{1,0:T(8,128)} %bitcast.4, f32[64,64]{1,0:T(8,128)} %bitcast.5, f32[64,64]{1,0:T(8,128)} %bitcast.6), custom_call_target="tpu_custom_call" | custom-call | tf_op jit(solution)/shard_map/influence/pallas_call | solution.py:452
  84.7 1.6 %broadcast_multiply_fusion = f32[32,1024]{1,0:T(8,128)} fusion(f32[32,1024]{1,0:T(8,128)} %influence.1), kind=kLoop, calls=%fused_computation | loop fusion | flops 32768 | bytes 262144 | tf_op jit(solution)/shard_map/mul | solution.py:452

commit v4 on v3

--- a/solution.py
+++ b/solution.py
@@ -25,6 +25,7 @@
 B = ((512, 1280), (2432, 3456))
 UP = ("0", "1", "2", "3")
 LAST = 6
+PITCH = 72
 DOWN = ("2", "3", "0", "1")
 
 
@@ -97,6 +98,12 @@
 
     load_g.wait()
 
+    def spread(ref, u, r):
+        for h in range(2):
+            for s in range(4):
+                start = pl.multiple_of((u * 8 + h * 4 + s) * PITCH, 8)
+                ref[pl.ds(start, 64), :] = r[s * 64 : s * 64 + 64, h * 128 : h * 128 + 128]
+
     def stage_a(u, c):
         base = pl.multiple_of(u * 512, 512)
         left = g_v[:, pl.ds(base, 256)]
@@ -105,15 +112,14 @@
             bdm[0], jnp.concatenate([left, right], axis=0), (((1,), (1,)), ((), ())), preferred_element_type=f32
         )
         r = both[:256] + both[256:]
-        y1[pl.ds(base, 256), :] = r[:, :128]
-        y1[pl.ds(base + 256, 256), :] = r[:, 128:]
+        spread(y1, u, r)
         return c
 
     def strided(ref, u):
         halves = []
         for h in range(2):
             halves.append(
-                jnp.concatenate([ref[pl.ds(u * 8 + h * 4 + s, 64, stride=64), :] for s in range(4)], axis=0)
+                jnp.concatenate([ref[pl.ds(u * 8 + h * 4 + s, 64, stride=PITCH), :] for s in range(4)], axis=0)
             )
         return jnp.concatenate(halves, axis=1)
 
@@ -122,8 +128,7 @@
         r = apply_basis(bdm[1], strided(y1, u))
         r = r * jnp.concatenate([inv[pl.ds(base, 256), :], inv[pl.ds(base + 256, 256), :]], axis=1)
         r = apply_basis(bdm[2], r)
-        y2[pl.ds(base, 256), :] = r[:, :128]
-        y2[pl.ds(base + 256, 256), :] = r[:, 128:]
+        spread(y2, u, r)
         return c
 
     def stage_d(u, c):
@@ -425,14 +430,6 @@
         src_ref=a_recv.at[pl.ds(0, 31)], dst_ref=a_recv.at[pl.ds(0, 31)], send_sem=a_ssem.at[0], recv_sem=a_rsem.at[0],
         device_id=up, device_id_type=MESH,
     )
-    dealt.wait_recv()
-    for m in range(8):
-        tiles = [a_recv[4 * m + n] for n in range(4)]
-        for k in range(4):
-            out_ref[8 * k : 8 * k + 8, 128 * m : 128 * m + 128] = jnp.concatenate(
-                [tile[:, 32 * k : 32 * k + 32] for tile in tiles], axis=1
-            )
-
     for copy in sends:
         copy.wait_send()
     for copy in id_copies:
@@ -442,6 +439,14 @@
         scattered(slot).wait_send()
         if slot != LAST:
             swap(slot).wait_send()
+    dealt.wait_recv()
+    for m in range(8):
+        tiles = [a_recv[4 * m + n] for n in range(4)]
+        for k in range(4):
+            out_ref[8 * k : 8 * k + 8, 128 * m : 128 * m + 128] = jnp.concatenate(
+                [tile[:, 32 * k : 32 * k + 32] for tile in tiles], axis=1
+            )
+
     dealt.wait_send()
 
 
@@ -458,8 +463,8 @@
             pltpu.VMEM((128, 4096), bf16),
             pltpu.VMEM((1024, 4096), bf16),
             pltpu.VMEM((8, 4096, 128), bf16),
-            pltpu.VMEM((4096, 128), f32),
-            pltpu.VMEM((4096, 128), f32),
+            pltpu.VMEM((64 * PITCH, 128), f32),
+            pltpu.VMEM((64 * PITCH, 128), f32),
             pltpu.VMEM((4096, 128), f32),
             pltpu.VMEM((4, 512, 256), bf16),
             pltpu.VMEM((8, 1024, 128), f32),
@@ -487,16 +492,16 @@
             dma((1,)),
         ],
         compiler_params=pltpu.CompilerParams(
-            collective_id=0, has_side_effects=True, vmem_limit_bytes=56 * 2**20
+            collective_id=0, has_side_effects=True, vmem_limit_bytes=48 * 2**20
         ),
         name="influence",
     )(
-        query_grads,
-        query_ids.reshape(1, 128),
-        train_feats,
-        basis_out[0],
-        basis_in[0],
-        eigen_vals[0],
+        *(
+            pltpu.with_memory_space_constraint(x, pltpu.HBM)
+            for x in (
+                query_grads, query_ids.reshape(1, 128), train_feats, basis_out[0], basis_in[0], eigen_vals[0]
+            )
+        )
     ) * (1.0 / math.sqrt(131072))
 
 

time: 86.4 us -> 84.3 us (0.976)
  Pallas kernels: 84.7 us -> 83.5 us
  other arithmetic: 1.57 us -> 0.67 us
    pallas_call x1, Pallas kernels: 84.7 us -> 83.5 us  [on_device(): pl.pallas_call(kernel, out_shape=jax.ShapeDtypeStruct((32, 1024), f32), i...]
    mul x1, other arithmetic: 1.57 us -> 0.67 us  [on_device(): pl.pallas_call(kernel, out_shape=jax.ShapeDtypeStruct((32, 1024), f32), i...]
where the time goes in v4:
time: 84.3 us; the launch traced here: 84.2 us
  Pallas kernels  83.5 us (99%)
    pallas_call x1, Pallas kernels, on_device(): pl.pallas_call(kernel, out_shape=jax.ShapeDtypeStruct((32, 1024), f32), i...  83.5 us

profile of v4, /device:TPU:1, one launch (start us, length us, event | category | flops | bytes accessed | tf_op | source)
XLA Modules:
  0.0 84.2 jit_solution(5847858911594940581)
XLA Ops:
  0.0 83.5 %influence.1 = f32[32,1024]{1,0:T(8,128)S(1)} custom-call(bf16[128,4096]{1,0:T(8,128)(2,1)} %g_hbm.1, s32[1,128]{1,0:T(1,128)} %bitcast.7, bf16[1024,4096]{1,0:T(8,128)(2,1)} %t_hbm.1, f32[64,64]{1,0:T(8,128)} %bitcast.4, f32[64,64]{1,0:T(8,128)} %bitcast.5, f32[64,64]{1,0:T(8,128)} %bitcast.6), custom_call_target="tpu_custom_call" | custom-call | tf_op jit(solution)/shard_map/influence/pallas_call | solution.py:457
  83.5 0.7 broadcast_multiply_fusion

commit v5 on v4

--- a/solution.py
+++ b/solution.py
@@ -56,7 +56,7 @@
 
 def kernel(
     g_hbm, ids_ref, t_hbm, bo_ref, bi_ref, eig_ref, out_ref,
-    g_v, t_v, q, y1, y2, inv, bdm, acc, cx, rs_send, rs_recv, zs, xs, ids, hot, a_send, a_recv,
+    g_v, t_v, q, y1, y2, inv, bdm, acc, cx, rs_send, rs_recv, zs, xs, ids, hot, a_send, a_round, a_recv,
     load_sem, q_send, q_recv, id_send, id_recv, cx_ssem, cx_rsem, rs_ssem, rs_rsem, xs_ssem, xs_rsem, a_ssem, a_rsem,
 ):
     group, layer = lax.axis_index("group"), lax.axis_index("layer")
@@ -78,12 +78,13 @@
         pl.semaphore_signal(barrier, inc=1, device_id=(lax.rem(group + k, 8), layer), device_id_type=MESH)
         return c
 
-    def greet_layer(k, c):
-        pl.semaphore_signal(barrier, inc=1, device_id=(group, lax.rem(layer + k, 32)), device_id_type=MESH)
+    def greet_layer(n, c):
+        to = lax.rem(layer + far(n, 32), 32)
+        pl.semaphore_signal(barrier, inc=1, device_id=(group, to), device_id_type=MESH)
         return c
 
+    lax.fori_loop(0, 31, greet_layer, 0, unroll=31)
     lax.fori_loop(1, 8, greet_group, 0, unroll=7)
-    lax.fori_loop(1, 32, greet_layer, 0, unroll=31)
     load_t.start()
 
     bo = diagonal(bo_ref[...])
@@ -269,14 +270,19 @@
         else:
             swap(slot).wait_recv()
             total = zs[slot, pl.ds(pl.multiple_of(xl * 32, 32), 32), :] + xs[slot]
-        placed = None
-        for half in split(total):
-            none = jnp.zeros_like(half)
-            spread = jnp.concatenate(
-                [jnp.concatenate([half if m == k else none for m in range(4)], axis=1) for k in range(4)], axis=0
+        spread = []
+        for half_total in split(total):
+            none = jnp.zeros_like(half_total)
+            spread.append(
+                jnp.concatenate(
+                    [jnp.concatenate([half_total if m == k else none for m in range(4)], axis=1) for k in range(4)],
+                    axis=0,
+                )
             )
-            term = lax.dot_general(hot[slot], spread, (((1,), (1,)), ((), ())), preferred_element_type=f32)
-            placed = term if placed is None else placed + term
+        placed = lax.dot_general(
+            jnp.concatenate([hot[slot], hot[slot]], axis=1), jnp.concatenate(spread, axis=1),
+            (((1,), (1,)), ((), ())), preferred_element_type=f32,
+        )
         placed = placed.reshape(32, 8, 128)
         a_send[...] = placed if slot == 0 else a_send[...] + placed
 
@@ -398,15 +404,12 @@
     half(6, (PIECES["a3"],), False, theirs)
     exchange(6).start()
     half(6, (PIECES["a3"],), False, mine)
-    zsum(7)
-    swap(7).start()
     collect(0)
+    collect(4)
     scatter(6)
-    zsum(5)
-    swap(5).start()
-    zsum(2)
-    swap(2).start()
-    collect(4)
+    for slot in (7, 5, 2):
+        zsum(slot)
+        swap(slot).start()
     collect(3)
     collect(1)
     collect(7)
@@ -415,17 +418,18 @@
     collect(6)
 
     place = core * 16 + me
+    a_round[...] = a_send[...].astype(bf16)
 
     def deal(n, c):
         to = lax.rem(layer + far(n, 32), 32)
         pltpu.make_async_remote_copy(
-            src_ref=a_send.at[to], dst_ref=a_recv.at[place], send_sem=a_ssem.at[0], recv_sem=a_rsem.at[0],
+            src_ref=a_round.at[to], dst_ref=a_recv.at[place], send_sem=a_ssem.at[0], recv_sem=a_rsem.at[0],
             device_id=(group, to), device_id_type=MESH,
         ).start()
         return c
 
     lax.fori_loop(0, 31, deal, 0, unroll=31)
-    a_recv[place] = a_send[layer]
+    a_recv[place] = a_round[layer]
     dealt = pltpu.make_async_remote_copy(
         src_ref=a_recv.at[pl.ds(0, 31)], dst_ref=a_recv.at[pl.ds(0, 31)], send_sem=a_ssem.at[0], recv_sem=a_rsem.at[0],
         device_id=up, device_id_type=MESH,
@@ -441,7 +445,7 @@
             swap(slot).wait_send()
     dealt.wait_recv()
     for m in range(8):
-        tiles = [a_recv[4 * m + n] for n in range(4)]
+        tiles = [a_recv[4 * m + n].astype(f32) for n in range(4)]
         for k in range(4):
             out_ref[8 * k : 8 * k + 8, 128 * m : 128 * m + 128] = jnp.concatenate(
                 [tile[:, 32 * k : 32 * k + 32] for tile in tiles], axis=1
@@ -476,7 +480,8 @@
             pltpu.VMEM((8, 1, 128), jnp.int32),
             pltpu.VMEM((8, 256, 512), bf16),
             pltpu.VMEM((32, 8, 128), f32),
-            pltpu.VMEM((32, 8, 128), f32),
+            pltpu.VMEM((32, 8, 128), bf16),
+            pltpu.VMEM((32, 8, 128), bf16),
             dma((2,)),
             dma((56,)),
             dma((64,)),

time: 84.3 us -> 83.6 us (level)
  no operation moved by 1% of the time
where the time goes in v5:
time: 83.6 us; the launch traced here: 83.5 us
  Pallas kernels  82.8 us (99%)
    pallas_call x1, Pallas kernels, on_device(): pl.pallas_call(kernel, out_shape=jax.ShapeDtypeStruct((32, 1024), f32), i...  82.8 us

profile of v5, /device:TPU:1, one launch (start us, length us, event | category | flops | bytes accessed | tf_op | source)
XLA Modules:
  0.0 83.5 jit_solution(18097152130461876711)
XLA Ops:
  0.0 82.8 %influence.1 = f32[32,1024]{1,0:T(8,128)S(1)} custom-call(bf16[128,4096]{1,0:T(8,128)(2,1)} %g_hbm.1, s32[1,128]{1,0:T(1,128)} %bitcast.7, bf16[1024,4096]{1,0:T(8,128)(2,1)} %t_hbm.1, f32[64,64]{1,0:T(8,128)} %bitcast.4, f32[64,64]{1,0:T(8,128)} %bitcast.5, f32[64,64]{1,0:T(8,128)} %bitcast.6), custom_call_target="tpu_custom_call" | custom-call | tf_op jit(solution)/shard_map/influence/pallas_call | solution.py:461
  82.8 0.7 broadcast_multiply_fusion

commit v6 on v5

--- a/solution.py
+++ b/solution.py
@@ -467,8 +467,8 @@
             pltpu.VMEM((128, 4096), bf16),
             pltpu.VMEM((1024, 4096), bf16),
             pltpu.VMEM((8, 4096, 128), bf16),
-            pltpu.VMEM((64 * PITCH, 128), f32),
-            pltpu.VMEM((64 * PITCH, 128), f32),
+            pltpu.VMEM((65 * PITCH, 128), f32),
+            pltpu.VMEM((65 * PITCH, 128), f32),
             pltpu.VMEM((4096, 128), f32),
             pltpu.VMEM((4, 512, 256), bf16),
             pltpu.VMEM((8, 1024, 128), f32),

time: 83.6 us -> 83.6 us (level)
  no operation moved by 1% of the time
where the time goes in v6:
time: 83.6 us; the launch traced here: 83.5 us
  Pallas kernels  82.8 us (99%)
    pallas_call x1, Pallas kernels, on_device(): pl.pallas_call(kernel, out_shape=jax.ShapeDtypeStruct((32, 1024), f32), i...  82.8 us

profile of v6, /device:TPU:1, one launch (start us, length us, event | category | flops | bytes accessed | tf_op | source)
XLA Modules:
  0.0 83.5 jit_solution(14664457999552614142)
XLA Ops:
  0.0 82.8 %influence.1 = f32[32,1024]{1,0:T(8,128)S(1)} custom-call(bf16[128,4096]{1,0:T(8,128)(2,1)} %g_hbm.1, s32[1,128]{1,0:T(1,128)} %bitcast.7, bf16[1024,4096]{1,0:T(8,128)(2,1)} %t_hbm.1, f32[64,64]{1,0:T(8,128)} %bitcast.4, f32[64,64]{1,0:T(8,128)} %bitcast.5, f32[64,64]{1,0:T(8,128)} %bitcast.6), custom_call_target="tpu_custom_call" | custom-call | tf_op jit(solution)/shard_map/influence/pallas_call | solution.py:461
  82.8 0.7 broadcast_multiply_fusion

commit v7 on v6

--- a/solution.py
+++ b/solution.py
@@ -399,11 +399,11 @@
     piece(6, "a2", False)
     piece(6, "b1", False)
     piece(6, "b3", False)
-    piece(6, "a1", False)
+    arrive(6, "a1")
     arrive(6, "a3")
-    half(6, (PIECES["a3"],), False, theirs)
+    half(6, (PIECES["a1"], PIECES["a3"]), False, theirs)
     exchange(6).start()
-    half(6, (PIECES["a3"],), False, mine)
+    half(6, (PIECES["a1"], PIECES["a3"]), False, mine)
     collect(0)
     collect(4)
     scatter(6)

time: 83.6 us -> 83.4 us (level)
  no operation moved by 1% of the time
where the time goes in v7:
time: 83.4 us; the launch traced here: 83.2 us
  Pallas kernels  82.5 us (99%)
    pallas_call x1, Pallas kernels, on_device(): pl.pallas_call(kernel, out_shape=jax.ShapeDtypeStruct((32, 1024), f32), i...  82.5 us

profile of v7, /device:TPU:1, one launch (start us, length us, event | category | flops | bytes accessed | tf_op | source)
XLA Modules:
  0.0 83.2 jit_solution(7370772940110897242)
XLA Ops:
  0.0 82.5 %influence.1 = f32[32,1024]{1,0:T(8,128)S(1)} custom-call(bf16[128,4096]{1,0:T(8,128)(2,1)} %g_hbm.1, s32[1,128]{1,0:T(1,128)} %bitcast.7, bf16[1024,4096]{1,0:T(8,128)(2,1)} %t_hbm.1, f32[64,64]{1,0:T(8,128)} %bitcast.4, f32[64,64]{1,0:T(8,128)} %bitcast.5, f32[64,64]{1,0:T(8,128)} %bitcast.6), custom_call_target="tpu_custom_call" | custom-call | tf_op jit(solution)/shard_map/influence/pallas_call | solution.py:461
  82.5 0.7 broadcast_multiply_fusion
